TPU v7x, 256 devices: a whole 4x4x8 slice. The times are simulated.
256 devices in a mesh: seq: 64 (over y, x, z_hi, core), head: 4 (over z_lo).
Axes of the slice: x: 4, y: 4, z: 8 (z_hi: 2, z_lo: 4; z = z_hi * 4 + z_lo), core: 2. Of those that a mesh axis runs over, the one named last changes fastest.
Arguments:
- query_rows: bfloat16 [16384, 5120], P('seq', 'head'), may hold values from -6 to 6
- key_rows: bfloat16 [16384, 5120], P('seq', 'head'), may hold values from -6 to 6
- value_rows: bfloat16 [16384, 5120], P('seq', 'head'), may hold values from -6 to 6
- attn_out: bfloat16 [16384, 5120], P('seq', 'head'), may hold values from -3 to 3
- log_total: float32 [40, 16384], P('head', 'seq'), as said below
- d_layer: bfloat16 [16384, 5120], P('seq', 'head'), may hold values from -6 to 6
- w_output: bfloat16 [5120, 5120], P('seq', 'head'), may hold values from -0.078125 to 0.078125
Outputs:
- d_query: bfloat16 [16384, 5120], P('seq', 'head')
- d_key: bfloat16 [16384, 5120], P('seq', 'head')
- d_value: bfloat16 [16384, 5120], P('seq', 'head')
Inputs may be any that keep to these rules, and one draw needn't show every extreme that they name: log_total[h, i] is the log of the sum of exp(score) over the keys allowed for row i of head h.
All inputs are finite; a program needn't handle non-finite values.
Results may differ from a plain program's by a relative error of at most 0.009.
Values may be sent and summed in bfloat16 or wider, within the bound.
A program may use at most 64 MiB of HBM per device.

v0:
```python
import jax
import jax.numpy as jnp
from jax import lax
from jax.sharding import PartitionSpec as P

HD = 128


big_negative = -1e30


def from_behind(block, axis, distance):
    devices = range(lax.axis_size(axis))
    route = [(i - distance, i) for i in devices if i - distance in devices]
    return lax.ppermute(block, axis, route)


def tile_grads(query_tile, dout_tile, log_tile, delta_tile, key_tile, value_tile, allowed):
    tile_rows = query_tile.shape[0]
    key_count = key_tile.shape[0]
    score_scale = HD ** (-0.5)
    query_heads = query_tile.reshape(tile_rows, -1, HD)
    dout_heads = dout_tile.reshape(tile_rows, -1, HD)
    key_heads = key_tile.reshape(key_count, -1, HD)
    value_heads = value_tile.reshape(key_count, -1, HD)
    raw_scores = (
        jnp.einsum("qhd,khd->hqk", query_heads, key_heads, preferred_element_type=jnp.float32)
        * score_scale
    )
    probs_full = jnp.exp(jnp.where(allowed[None], raw_scores, big_negative) - log_tile[:, :, None])
    probs_low = probs_full.astype(jnp.bfloat16)
    grad_value = jnp.einsum(
        "hqk,qhd->khd", probs_low, dout_heads, preferred_element_type=jnp.float32
    )
    grad_probs = jnp.einsum(
        "qhd,khd->hqk", dout_heads, value_heads, preferred_element_type=jnp.float32
    )
    scores_low = (probs_full * (grad_probs - delta_tile[:, :, None])).astype(jnp.bfloat16)
    grad_query = (
        jnp.einsum("hqk,khd->qhd", scores_low, key_heads, preferred_element_type=jnp.float32)
        * score_scale
    )
    grad_key = (
        jnp.einsum("hqk,qhd->khd", scores_low, query_heads, preferred_element_type=jnp.float32)
        * score_scale
    )
    return (
        grad_query.reshape(tile_rows, -1),
        grad_key.reshape(key_count, -1),
        grad_value.reshape(key_count, -1),
    )


def block_grads(query_blk, dout_blk, log_blk, delta_blk, key_blk, value_blk, diagonal, live):
    block_rows, col_count = query_blk.shape
    tile = min(512, block_rows)
    lower = jnp.arange(tile, dtype=jnp.int32)[None, :] <= jnp.arange(tile, dtype=jnp.int32)[:, None]
    whole = jnp.broadcast_to(live, (tile, tile))
    query_parts = [jnp.zeros((tile, col_count), jnp.float32)]
    key_parts = [jnp.zeros((tile, col_count), jnp.float32)]
    value_parts = [jnp.zeros((tile, col_count), jnp.float32)]
    allowed = lower if diagonal else whole
    tile_out = tile_grads(query_blk, dout_blk, log_blk, delta_blk, key_blk, value_blk, allowed)
    query_parts[0] = tile_out[0]
    key_parts[0] = tile_out[1]
    value_parts[0] = tile_out[2]
    return (query_parts[0], key_parts[0], value_parts[0])


def on_device(query_rows, key_rows, value_rows, attn_out, log_total, d_layer, w_output):
    seq_index = lax.axis_index("seq")
    tok_rows = query_rows.shape[0]
    col_count = query_rows.shape[1]
    head_count = col_count // HD
    partial_terms = lax.dot_general(
        d_layer,
        lax.all_gather(w_output, "seq", axis=0, tiled=True),
        (((1,), (1,)), ((), ())),
        preferred_element_type=jnp.float32,
    )
    d_attn = lax.psum_scatter(partial_terms, "head", scatter_dimension=1, tiled=True).astype(
        jnp.bfloat16
    )
    products = d_attn.astype(jnp.float32) * attn_out.astype(jnp.float32)
    row_delta = jnp.sum(products.reshape(tok_rows, head_count, HD), axis=2).T
    always_live = jnp.array(True)
    own_part = block_grads(
        query_rows, d_attn, log_total, row_delta, key_rows, value_rows, True, always_live
    )
    key_prev, value_prev = from_behind((key_rows, value_rows), "seq", 1)
    cross_part = block_grads(
        query_rows, d_attn, log_total, row_delta, key_prev, value_prev, False, seq_index > 0
    )
    key_back, value_back = from_behind((cross_part[1], cross_part[2]), "seq", -1)
    grad_query = own_part[0] + cross_part[0]
    grad_key = own_part[1] + key_back
    grad_value = own_part[2] + value_back
    d_query = grad_query.astype(jnp.bfloat16)
    d_key = grad_key.astype(jnp.bfloat16)
    d_value = grad_value.astype(jnp.bfloat16)
    return (d_query, d_key, d_value)


def solution(mesh):
    return jax.shard_map(
        on_device,
        mesh=mesh,
        in_specs=(
            P("seq", "head"),
            P("seq", "head"),
            P("seq", "head"),
            P("seq", "head"),
            P("head", "seq"),
            P("seq", "head"),
            P("seq", "head"),
        ),
        out_specs=(P("seq", "head"), P("seq", "head"), P("seq", "head")),
        check_vma=False,
    )
```

profile of v0, /device:TPU:7, one launch (start us, length us, event | category | flops | bytes accessed | tf_op | source)
XLA Modules:
  0.0 382.5 jit_solution(12956504142721185176)
XLA Ops:
  7.2 0.0 copy-start
  7.2 0.0 all-gather.2.cloned.1.call-start
  7.2 0.7 all-gather.2.cloned.1.call-update
  7.9 0.0 reduce-scatter.2.cloned.1.call-start
  8.0 143.0 %all-gather.2.cloned.1.call-done = bf16[5120,1280]{1,0:T(8,128)(2,1)} async-done(((bf16[80,1280]{1,0:T(8,128)(2,1)}), bf16[5120,1280]{1,0:T(8,128)(2,1)}) %all-gather.2.cloned.1.call-update) | async-done | bytes 13107216 | tf_op jit(solution)/shard_map/all_gather | solution.py:77
  151.0 0.0 copy-done
  151.0 14.8 %fusion.21 = f32[256,5120]{1,0:T(8,128)} fusion(bf16[256,1280]{1,0:T(8,128)(2,1)S(1)} %copy-done, bf16[5120,1280]{1,0:T(8,128)(2,1)} %all-gather.2.cloned.1.call-done), kind=kOutput, calls=%fused_computation.30 | convolution fusion | flops 3355443200 | bytes 19005440 | tf_op jit(solution)/shard_map/dot_general | solution.py:75
  165.8 0.0 copy-start.8
  165.8 0.0 reduce-scatter.2.cloned.1.call-update
  165.8 1.1 copy-done.8
  166.9 0.0 copy-start.9
  166.9 0.2 copy.28
  167.1 1.9 collective-permute-start
  169.1 0.0 copy-done.9
  169.1 1.1 copy.32
  170.1 1.9 collective-permute-start.1
  172.1 1.5 copy.27
  173.6 2.1 fusion.20
  175.7 14.1 %collective-permute-done = bf16[256,1280]{0,1:T(8,128)(2,1)S(1)} collective-permute-done((bf16[256,1280]{0,1:T(8,128)(2,1)S(1)}, bf16[256,1280]{0,1:T(8,128)(2,1)S(1)}, u32[]{:S(2)}, u32[]{:S(2)}) %collective-permute-start) | collective-permute-done | bytes 655392 | tf_op jit(solution)/shard_map/ppermute | solution.py:15
  189.8 0.0 copy-start.7
  189.8 2.1 fusion.23
  191.8 0.0 copy-done.7
  191.8 91.8 %reduce-scatter.2.cloned.1.call-done = f32[256,1280]{1,0:T(8,128)} async-done(((f32[256,5120]{1,0:T(8,128)}), f32[256,1280]{1,0:T(8,128)}) %reduce-scatter.2.cloned.1.call-update) | async-done | bytes 1310736 | tf_op jit(solution)/shard_map/reduce_scatter | solution.py:81
  283.7 2.5 convert_multiply_fusion
  286.2 1.5 copy.35
  287.7 0.0 copy-start.10
  287.7 1.3 copy.31
  289.0 0.0 copy-done.10
  289.0 3.6 fusion.4
  292.6 2.8 copy.44
  295.4 1.4 reduce_sum.9
  296.8 0.0 collective-permute-done.1
  296.8 2.8 multiply_convert_fusion
  299.6 0.0 copy-start.5
  299.6 1.6 convolution_multiply_fusion
  301.2 0.0 copy-done.5
  301.2 2.8 copy.42
  304.0 0.0 copy-start.1
  304.0 2.5 collective-permute-start.2
  306.5 8.3 %collective-permute-start.3 = (f32[256,1280]{1,0:T(8,128)}, f32[256,1280]{1,0:T(8,128)}, u32[]{:S(2)}, u32[]{:S(2)}) collective-permute-start(f32[256,1280]{1,0:T(8,128)} %copy.44), channel_id=1, source_target_pairs={{4,0},{8,4},{12,8},{16,12},{20,16},{24,20},{28,24},{32,28},{36,32}... | collective-permute-start | bytes 3932168 | tf_op jit(solution)/shard_map/ppermute | solution.py:15
  314.8 3.5 fusion.6
  318.4 0.0 copy-done.1
  318.4 2.4 multiply_convert_fusion.1
  320.8 0.0 copy-start.2
  320.8 1.6 fusion.22
  322.4 0.0 copy-done.2
  322.4 0.0 copy-start.6
  322.4 2.9 copy.45
  325.3 0.0 copy-done.6
  325.3 2.1 fusion.3
  327.4 0.0 copy-start.3
  327.4 1.1 copy.46
  328.5 0.5 copy-done.3
  329.0 1.4 convolution_multiply_fusion.1
  330.4 0.0 copy-start.4
  330.4 1.8 copy.43
  332.2 38.9 %collective-permute-done.3 = f32[256,1280]{1,0:T(8,128)} collective-permute-done((f32[256,1280]{1,0:T(8,128)}, f32[256,1280]{1,0:T(8,128)}, u32[]{:S(2)}, u32[]{:S(2)}) %collective-permute-start.3) | collective-permute-done | bytes 1310752 | tf_op jit(solution)/shard_map/ppermute | solution.py:15
  371.1 0.0 copy-done.4
  371.1 2.3 add_convert_fusion
  373.4 0.0 collective-permute-done.2
  373.4 2.3 add_convert_fusion.1
  (1 shorter events, 0.0 us)
Async XLA Ops:
  7.2 143.8 %copy-start = (bf16[256,1280]{1,0:T(8,128)(2,1)S(1)}, bf16[256,1280]{1,0:T(8,128)(2,1)}, u32[]{:S(2)}) copy-start(bf16[256,1280]{1,0:T(8,128)(2,1)} %param.12) | copy-start | bytes 1966084
  7.2 143.8 %all-gather.2.cloned.1.call-start = ((), (), s32[]{:S(2)}) async-start(), calls=%async_computation.1 | async-start | bytes 13312000 | tf_op jit(solution)/shard_map/all_gather | solution.py:77
  7.9 275.8 %reduce-scatter.2.cloned.1.call-start = ((), (), s32[]{:S(2)}) async-start(), calls=%async_computation.2 | async-start | bytes 6553600 | tf_op jit(solution)/shard_map/reduce_scatter | solution.py:81
  165.8 1.1 copy-start.8
  166.9 2.2 copy-start.9
  167.1 22.6 %collective-permute-start = (bf16[256,1280]{0,1:T(8,128)(2,1)S(1)}, bf16[256,1280]{0,1:T(8,128)(2,1)S(1)}, u32[]{:S(2)}, u32[]{:S(2)}) collective-permute-start(bf16[256,1280]{0,1:T(8,128)(2,1)S(1)} %copy.28), channel_id=1, source_target_pairs={{0,4},{4,8},{8,12},{12,16},{16,20},{20,24},{24,28},{28,32},{32,36}... | collective-permute-start | bytes 1966088 | tf_op jit(solution)/shard_map/ppermute | solution.py:15
  170.1 126.7 %collective-permute-start.1 = (bf16[256,1280]{0,1:T(8,128)(2,1)}, bf16[256,1280]{0,1:T(8,128)(2,1)}, u32[]{:S(2)}, u32[]{:S(2)}) collective-permute-start(bf16[256,1280]{0,1:T(8,128)(2,1)} %copy.32), channel_id=1, source_target_pairs={{0,4},{4,8},{8,12},{12,16},{16,20},{20,24},{24,28},{28,32},{32,36}... | collective-permute-start | bytes 1966088 | tf_op jit(solution)/shard_map/ppermute | solution.py:15
  189.8 2.1 copy-start.7
  287.7 1.3 copy-start.10
  299.6 1.6 copy-start.5
  304.0 14.4 %copy-start.1 = (f32[10,256,256]{2,1,0:T(8,128)S(1)}, f32[10,256,256]{2,1,0:T(8,128)}, u32[]{:S(2)}) copy-start(f32[10,256,256]{2,1,0:T(8,128)} %fusion.20) | copy-start | bytes 7864324
  304.0 69.4 %collective-permute-start.2 = (f32[256,1280]{1,0:T(8,128)}, f32[256,1280]{1,0:T(8,128)}, u32[]{:S(2)}, u32[]{:S(2)}) collective-permute-start(f32[256,1280]{1,0:T(8,128)} %copy.42), channel_id=1, source_target_pairs={{4,0},{8,4},{12,8},{16,12},{20,16},{24,20},{28,24},{32,28},{36,32}... | collective-permute-start | bytes 3932168 | tf_op jit(solution)/shard_map/ppermute | solution.py:15
  306.5 64.6 %collective-permute-start.3 = (f32[256,1280]{1,0:T(8,128)}, f32[256,1280]{1,0:T(8,128)}, u32[]{:S(2)}, u32[]{:S(2)}) collective-permute-start(f32[256,1280]{1,0:T(8,128)} %copy.44), channel_id=1, source_target_pairs={{4,0},{8,4},{12,8},{16,12},{20,16},{24,20},{28,24},{32,28},{36,32}... | collective-permute-start | bytes 3932168 | tf_op jit(solution)/shard_map/ppermute | solution.py:15
  320.8 1.6 copy-start.2
  322.4 2.9 copy-start.6
  327.4 1.6 copy-start.3
  330.4 40.7 %copy-start.4 = (f32[256,1280]{1,0:T(8,128)S(1)}, f32[256,1280]{1,0:T(8,128)}, u32[]{:S(2)}) copy-start(f32[256,1280]{1,0:T(8,128)} %copy.45) | copy-start | bytes 3932164
Sparse Core Ops, SparseCore 0:
  11.5 139.4 all-gather.1
  165.9 117.6 reduce-scatter.1
where the time goes:
time: 383 us
  waiting for transfers between devices  289 us (75%)
  matrix products  38 us (10%)
  local copies, waits for them, and re-layouts  18.6 us (5%)
  starting transfers between devices  14.7 us (4%)
  between operations  14.2 us (4%)
  other arithmetic  8.49 us (2%)
    all_gather x1, waiting for transfers between devices, on_device(): lax.all_gather(w_output, 'seq', axis=0, tiled=True)  143 us
    reduce_scatter x1, waiting for transfers between devices, on_device(): lax.psum_scatter(partial_terms, 'head', scatter_dimension=1, tiled=True)  91.8 us
    ppermute x4, waiting for transfers between devices, from_behind(): return lax.ppermute(block, axis, route)  53 us
    dot_general x1, matrix products, on_device(): lax.dot_general(d_layer, lax.all_gather(w_output, 'seq', axis=0, tiled=Tr...  14.8 us
    ppermute x4, starting transfers between devices, from_behind(): return lax.ppermute(block, axis, route)  14.6 us
  transfers between devices with their start and end apart: 6, of which 4 were waited for; matrix products, arithmetic and copies ran while one was open for 10% of the time, Pallas kernels for 0%

commit v1 on v0

v1 whole, which is shorter than its diff:
```python
import functools

import jax
import jax.numpy as jnp
from jax import lax
from jax.experimental import pallas as pl
from jax.experimental.pallas import tpu as pltpu
from jax.sharding import PartitionSpec as P

HD = 128
SCALE = HD ** (-0.5)
MASKED = -1e30
CHUNK = 256
MESH = pl.DeviceIdType.MESH
NT = (((1,), (1,)), ((), ()))
NN = (((1,), (0,)), ((), ()))
TN = (((0,), (0,)), ((), ()))


def dot(a, b, dims):
    return lax.dot_general(a, b, dims, preferred_element_type=jnp.float32)


def kernel(
    q_hbm, k_hbm, v_hbm, ao_hbm, log_hbm, dl_hbm, w_hbm,
    dq_ref, dk_ref, dv_ref,
    wbuf, dl, q, k, v, ao, logs, q_next, log_next,
    keep, send1, recv1, send2, recv2, do, do_next, delta, delta_next,
    dq_acc, dk_acc, dv_acc, dq_send, dq_recv,
    local_sem, w_send, w_recv, one_send, one_recv, two_send, two_recv,
    q_send, q_rsem, do_send, do_rsem, delta_send, delta_rsem, back_send, back_rsem,
):
    seq = lax.axis_index("seq")
    zlo = lax.axis_index("head")
    core = lax.rem(seq, 2)
    zhi = lax.rem(seq // 2, 2)
    x = lax.rem(seq // 4, 4)
    y = seq // 16
    shard = w_hbm.shape[0]
    chunks = q.shape[1] // CHUNK
    heads = CHUNK // HD

    def slot(yy, xx, hh, cc):
        return ((lax.rem(yy + 4, 4) * 4 + lax.rem(xx + 4, 4)) * 2 + hh) * 2 + cc

    sibling = (slot(y, x, zhi, 1 - core), zlo)
    far = (slot(y, x, 1 - zhi, core), zlo)
    before = (lax.rem(seq + 63, 64), zlo)
    after = (lax.rem(seq + 1, 64), zlo)
    flip1 = zlo + 1 - 2 * lax.rem(zlo, 2)
    flip2 = lax.rem(zlo + 2, 4)
    side1 = (seq, flip1)
    side2 = (seq, flip2)

    def at(f, i, j):
        return slot(y + f * i + (1 - f) * j, x + (1 - f) * i + f * j, f, core)

    def near(f, i, j):
        return (slot(y + f * i + (1 - f) * j, x + (1 - f) * i + f * j, zhi, core), zlo)

    loads = [
        pltpu.make_async_copy(src, dst, local_sem.at[n])
        for n, (src, dst) in enumerate(
            [(dl_hbm, dl), (q_hbm, q), (k_hbm, k), (v_hbm, v), (ao_hbm, ao), (log_hbm, logs)]
        )
    ]

    def w_rows(s):
        return wbuf.at[pl.ds(pl.multiple_of(s * shard, 16), shard)]

    own = pltpu.make_async_copy(w_hbm, w_rows(seq), w_recv.at[seq])
    own.start()
    for c in loads:
        c.start()

    barrier = pltpu.get_barrier_semaphore()
    partners = [sibling, far, before, after, side1, side2]
    for d in (1, -1):
        partners += [near(0, d, 0), near(0, 0, d)]
    for p in partners:
        pl.semaphore_signal(barrier, inc=1, device_id=p, device_id_type=MESH)
    pl.semaphore_wait(barrier, len(partners))

    w_sends = []

    def w_copy(s, device, n):
        return pltpu.make_async_remote_copy(
            w_rows(s), w_rows(s), w_send.at[n], w_recv.at[s],
            device_id=device, device_id_type=MESH,
        )

    def send_w(s, device):
        c = w_copy(s, device, len(w_sends))
        c.start()
        w_sends.append(c)

    def wait_w(s):
        w_copy(s, sibling, 0).wait_recv()

    own.wait()
    send_w(seq, far)
    zf, zg = zhi, 1 - zhi

    def begin(f):
        s = at(f, 0, 0)
        for d in (1, -1):
            send_w(s, near(f, d, 0))
            send_w(s, near(f, 0, d))
        send_w(s, sibling)

    def spread(f, i):
        s = at(f, i, 0)
        for d in (1, -1):
            send_w(s, near(f, 0, d))
        send_w(s, sibling)

    def first_near(f):
        wait_w(at(f, 1, 0))
        wait_w(at(f, -1, 0))
        step = 1 - 2 * core
        send_w(at(f, -step, 0), near(f, step, 0))
        spread(f, 1)
        spread(f, -1)

    def first_far(f):
        wait_w(at(f, 2, 0))
        spread(f, 2)

    def second_near(f, i):
        for d in (1, -1):
            wait_w(at(f, i, d))
        d = 1 if i in (0, 1) else -1
        send_w(at(f, i, -d), near(f, 0, d))
        for d in (1, -1):
            send_w(at(f, i, d), sibling)

    def second_far(f, i):
        wait_w(at(f, i, 2))
        send_w(at(f, i, 2), sibling)

    def cross_wait(h):
        for xx in range(4):
            for hh in range(2):
                wait_w(slot(h, xx, hh, 1 - core))

    def one_copy(j, t):
        return pltpu.make_async_remote_copy(
            send1.at[j, t], recv1.at[j, t], one_send.at[j, t], one_recv.at[j, t],
            device_id=side1, device_id_type=MESH,
        )

    def two_copy(t):
        return pltpu.make_async_remote_copy(
            send2.at[t], recv2.at[t], two_send.at[t], two_recv.at[t],
            device_id=side2, device_id_type=MESH,
        )

    def group(d):
        h = lax.rem(y + d + 4, 4)
        cross_wait(h)
        mine = lax.rem(h + zlo, 2) == 0

        def product(t):
            rows = pl.ds(pl.multiple_of(h * (chunks * CHUNK) + t * CHUNK, CHUNK), CHUNK)
            return dot(dl[...], wbuf[rows, :], NT)

        @pl.when(mine)
        def _():
            j = jnp.where(h == zlo, 0, 1)

            def body(t, carry):
                keep[j, t] = product(t)
                return carry

            lax.fori_loop(0, chunks, body, 0)

        @pl.when(jnp.logical_not(mine))
        def _():
            j = jnp.where(h == flip1, 0, 1)

            def body(t, carry):
                send1[j, t] = product(t).astype(jnp.bfloat16)
                one_copy(j, t).start()
                return carry

            lax.fori_loop(0, chunks, body, 0)

    begin(zf)
    first_near(zf)
    wait_w(at(zg, 0, 0))
    begin(zg)
    q_copy = pltpu.make_async_remote_copy(
        q, q_next, q_send.at[0], q_rsem.at[0], device_id=before, device_id_type=MESH
    )
    log_copy = pltpu.make_async_remote_copy(
        logs, log_next, q_send.at[1], q_rsem.at[1], device_id=before, device_id_type=MESH
    )
    for c in loads:
        c.wait()
    q_copy.start()
    log_copy.start()
    first_far(zf)
    first_near(zg)
    second_near(zf, 0)
    first_far(zg)
    second_near(zf, 1)
    second_near(zg, 0)
    second_near(zf, -1)
    second_near(zg, 1)
    second_near(zf, 2)
    second_near(zg, -1)
    second_far(zf, 0)
    second_far(zg, 0)
    group(0)
    second_near(zg, 2)
    second_far(zf, 1)
    second_far(zg, 1)
    group(1)
    second_far(zf, -1)
    second_far(zg, -1)
    group(-1)
    second_far(zf, 2)
    second_far(zg, 2)
    group(2)

    def combine(t, carry):
        one_copy(1, t).wait_recv()
        send2[t] = (keep[1, t] + recv1[1, t].astype(jnp.float32)).astype(jnp.bfloat16)
        two_copy(t).start()
        return carry

    lax.fori_loop(0, chunks, combine, 0)

    def do_copy(t):
        return pltpu.make_async_remote_copy(
            do.at[t], do_next.at[t], do_send.at[t], do_rsem.at[t],
            device_id=before, device_id_type=MESH,
        )

    def delta_copy(t):
        return pltpu.make_async_remote_copy(
            delta.at[t], delta_next.at[t], delta_send.at[t], delta_rsem.at[t],
            device_id=before, device_id_type=MESH,
        )

    def back_copy(t):
        return pltpu.make_async_remote_copy(
            dq_send.at[t], dq_recv.at[t], back_send.at[t], back_rsem.at[t],
            device_id=after, device_id_type=MESH,
        )

    def cols(t, n):
        return pl.ds(pl.multiple_of(t * CHUNK + n * HD, HD), HD)

    def finish(t, carry):
        one_copy(0, t).wait_recv()
        two_copy(t).wait_recv()
        total = keep[0, t] + recv1[0, t].astype(jnp.float32) + recv2[t].astype(jnp.float32)
        do[t] = total.astype(jnp.bfloat16)
        do_copy(t).start()
        for n in range(heads):
            prod = do[t, :, n * HD:(n + 1) * HD].astype(jnp.float32) * ao[:, cols(t, n)].astype(jnp.float32)
            row = jnp.sum(prod.T, axis=0, keepdims=True)
            delta[t, n * 8:(n + 1) * 8, :] = jnp.broadcast_to(row, (8, row.shape[1]))
        delta_copy(t).start()
        return carry

    lax.fori_loop(0, chunks, finish, 0)

    rows_i = q.shape[0]
    key_at = lax.broadcasted_iota(jnp.int32, (rows_i, rows_i), 0)
    query_at = lax.broadcasted_iota(jnp.int32, (rows_i, rows_i), 1)

    def head_grads(qh, kh, vh, doh, log_row, delta_row, allowed):
        score = dot(kh, qh, NT) * SCALE - log_row
        probs = jnp.exp(jnp.where(allowed, score, MASKED))
        g_value = dot(probs.astype(jnp.bfloat16), doh, NN)
        g_probs = dot(vh, doh, NT)
        low = (probs * (g_probs - delta_row)).astype(jnp.bfloat16)
        g_key = dot(low, qh, NN) * SCALE
        g_query = dot(low, kh, TN) * SCALE
        return g_query, g_key, g_value

    def diagonal(t, carry):
        for n in range(heads):
            c = cols(t, n)
            part = slice(n * HD, (n + 1) * HD)
            g = head_grads(
                q[:, c], k[:, c], v[:, c], do[t, :, part],
                logs[pl.ds(t * heads + n, 1), :], delta[t, n * 8:n * 8 + 1, :],
                key_at <= query_at,
            )
            dq_acc[t, :, part], dk_acc[t, :, part], dv_acc[t, :, part] = g
        return carry

    lax.fori_loop(0, chunks, diagonal, 0)

    q_copy.wait_recv()
    log_copy.wait_recv()
    limit = jnp.where(seq < 63, rows_i, 0)

    def crossing(t, carry):
        do_copy(t).wait_recv()
        delta_copy(t).wait_recv()
        for n in range(heads):
            c = cols(t, n)
            part = slice(n * HD, (n + 1) * HD)
            g_query, g_key, g_value = head_grads(
                q_next[:, c], k[:, c], v[:, c], do_next[t, :, part],
                log_next[pl.ds(t * heads + n, 1), :], delta_next[t, n * 8:n * 8 + 1, :],
                key_at < limit,
            )
            dq_send[t, :, part] = g_query.astype(jnp.bfloat16)
            dk_ref[:, c] = (dk_acc[t, :, part] + g_key).astype(jnp.bfloat16)
            dv_ref[:, c] = (dv_acc[t, :, part] + g_value).astype(jnp.bfloat16)
        back_copy(t).start()
        return carry

    lax.fori_loop(0, chunks, crossing, 0)

    def close(t, carry):
        back_copy(t).wait_recv()
        c = pl.ds(pl.multiple_of(t * CHUNK, CHUNK), CHUNK)
        dq_ref[:, c] = (dq_acc[t] + dq_recv[t].astype(jnp.float32)).astype(jnp.bfloat16)
        return carry

    lax.fori_loop(0, chunks, close, 0)

    for c in w_sends:
        c.wait_send()
    q_copy.wait_send()
    log_copy.wait_send()

    def drain(t, carry):
        one_copy(0, t).wait_send()
        one_copy(1, t).wait_send()
        two_copy(t).wait_send()
        do_copy(t).wait_send()
        delta_copy(t).wait_send()
        back_copy(t).wait_send()
        return carry

    lax.fori_loop(0, chunks, drain, 0)


def on_device(query_rows, key_rows, value_rows, attn_out, log_total, d_layer, w_output):
    rows, width = query_rows.shape
    n_heads = log_total.shape[0]
    chunks = width // CHUNK
    seqs = lax.axis_size("seq")
    bf, f32 = jnp.bfloat16, jnp.float32
    full = (rows, width)
    cut = (chunks, rows, CHUNK)
    dma = pltpu.SemaphoreType.DMA
    vm = pltpu.VMEM
    scratch = [
        vm((w_output.shape[0] * seqs, width), bf),
        vm(full, bf), vm(full, bf), vm(full, bf), vm(full, bf), vm(full, bf),
        vm((n_heads, rows), f32), vm(full, bf), vm((n_heads, rows), f32),
        vm((2,) + cut, f32), vm((2,) + cut, bf), vm((2,) + cut, bf),
        vm(cut, bf), vm(cut, bf), vm(cut, bf), vm(cut, bf),
        vm((chunks, 16, rows), f32), vm((chunks, 16, rows), f32),
        vm(cut, f32), vm(cut, f32), vm(cut, f32), vm(cut, bf), vm(cut, bf),
        dma((6,)), dma((64,)), dma((64,)), dma((2, chunks)), dma((2, chunks)),
        dma((chunks,)), dma((chunks,)), dma((2,)), dma((2,)),
        dma((chunks,)), dma((chunks,)), dma((chunks,)), dma((chunks,)),
        dma((chunks,)), dma((chunks,)),
    ]
    out = jax.ShapeDtypeStruct(full, bf)
    return pl.pallas_call(
        kernel,
        out_shape=(out, out, out),
        in_specs=[pl.BlockSpec(memory_space=pl.ANY)] * 7,
        out_specs=[pl.BlockSpec(memory_space=pltpu.VMEM)] * 3,
        scratch_shapes=scratch,
        compiler_params=pltpu.CompilerParams(
            collective_id=0, has_side_effects=True, vmem_limit_bytes=56 * 2**20
        ),
    )(query_rows, key_rows, value_rows, attn_out, log_total, d_layer, w_output)


def solution(mesh):
    spec = P("seq", "head")
    return jax.shard_map(
        on_device,
        mesh=mesh,
        in_specs=(spec, spec, spec, spec, P("head", "seq"), spec, spec),
        out_specs=(spec, spec, spec),
        check_vma=False,
    )
```

time: 383 us -> 166 us (0.43)
  the two profiles are of different devices: /device:TPU:7 before, /device:TPU:10 now
where the time goes in v1:
time: 166 us
  Pallas kernels  161 us (97%)
  local copies, waits for them, and re-layouts  4.19 us (3%)
    pallas_call x1, Pallas kernels, on_device(): pl.pallas_call(kernel, out_shape=(out, out, out), in_specs=[pl.BlockSpec(...  161 us
    unnamed x7, local copies, waits for them, and re-layouts  4.19 us

profile of v1, /device:TPU:10, one launch (start us, length us, event | category | flops | bytes accessed | tf_op | source)
XLA Modules:
  0.0 165.8 jit_solution(1947034847058820786)
XLA Ops:
  0.6 160.9 %shard_map.94 = (bf16[256,1280]{1,0:T(8,128)(2,1)}, bf16[256,1280]{1,0:T(8,128)(2,1)}, bf16[256,1280]{1,0:T(8,128)(2,1)}) custom-call(bf16[256,1280]{1,0:T(8,128)(2,1)} %q_hbm.1, bf16[256,1280]{1,0:T(8,128)(2,1)} %k_hbm.1, bf16[256,1280]{1,0:T(8,128)(2,1)} %v_hbm.1, bf16[256,1280]{1,0:T(8,128)(2,1)} %ao_hbm.1, f32[10,256]{1,0:T(8,128)} %log_hbm.1, ...), custom_call_target="tpu_custom_call" | custom-call | tf_op jit(solution)/shard_map/pallas_call | solution.py:370
  161.6 0.0 copy-start.1
  161.6 2.0 %copy.13 = bf16[256,1280]{1,0:T(8,128)(2,1)} copy(bf16[256,1280]{1,0:T(8,128)(2,1)} %get-tuple-element.6) | data formatting | bytes 1310720
  163.6 0.0 copy-done.1
  163.6 0.0 copy-start
  163.6 0.8 copy.14
  164.5 0.5 copy-done
  164.9 0.8 copy.15
Async XLA Ops:
  161.6 2.0 %copy-start.1 = (bf16[256,1280]{1,0:T(8,128)(2,1)S(1)}, bf16[256,1280]{1,0:T(8,128)(2,1)}, u32[]{:S(2)}) copy-start(bf16[256,1280]{1,0:T(8,128)(2,1)} %get-tuple-element.7) | copy-start | bytes 1966084
  163.6 1.3 copy-start

commit v2 on v1

v2 whole, which is shorter than its diff:
```python
import functools

import jax
import jax.numpy as jnp
from jax import lax
from jax.experimental import pallas as pl
from jax.experimental.pallas import tpu as pltpu
from jax.sharding import PartitionSpec as P

HD = 128
SCALE = HD ** (-0.5)
MASKED = -1e30
CHUNK = 256
MESH = pl.DeviceIdType.MESH
NT = (((1,), (1,)), ((), ()))
NN = (((1,), (0,)), ((), ()))
TN = (((0,), (0,)), ((), ()))


def dot(a, b, dims):
    return lax.dot_general(a, b, dims, preferred_element_type=jnp.float32)


def kernel(
    q_hbm, k_hbm, v_hbm, ao_hbm, log_hbm, dl_hbm, w_hbm,
    dq_ref, dk_ref, dv_ref,
    wbuf, dl, q, k, v, ao, ao_t, logs, q_next, log_next,
    keep, send1, recv1, send2, recv2, do, do_next, delta, delta_next,
    dq_acc, dk_acc, dv_acc, dq_send, dq_recv,
    local_sem, w_send, w_recv, one_send, one_recv, two_send, two_recv,
    q_send, q_rsem, do_send, do_rsem, delta_send, delta_rsem, back_send, back_rsem,
):
    seq = lax.axis_index("seq")
    zlo = lax.axis_index("head")
    core = lax.rem(seq, 2)
    zhi = lax.rem(seq // 2, 2)
    x = lax.rem(seq // 4, 4)
    y = seq // 16
    shard = w_hbm.shape[0]
    block = 2 * shard
    width = q.shape[1]
    chunks = width // CHUNK
    heads = CHUNK // HD

    def slot(yy, xx, hh, cc):
        return ((lax.rem(yy + 4, 4) * 4 + lax.rem(xx + 4, 4)) * 2 + hh) * 2 + cc

    sibling = (slot(y, x, zhi, 1 - core), zlo)
    far = (slot(y, x, 1 - zhi, core), zlo)
    before = (lax.rem(seq + 63, 64), zlo)
    after = (lax.rem(seq + 1, 64), zlo)
    flip1 = zlo + 1 - 2 * lax.rem(zlo, 2)
    flip2 = lax.rem(zlo + 2, 4)
    side1 = (seq, flip1)
    side2 = (seq, flip2)

    def place(i, j):
        return y + core * i + (1 - core) * j, x + (1 - core) * i + core * j

    def at(f, i, j):
        yy, xx = place(i, j)
        return slot(yy, xx, f, core)

    def near(i, j):
        yy, xx = place(i, j)
        return (slot(yy, xx, zhi, core), zlo)

    loads = [
        pltpu.make_async_copy(src, dst, local_sem.at[n])
        for n, (src, dst) in enumerate(
            [(dl_hbm, dl), (q_hbm, q), (k_hbm, k), (v_hbm, v), (ao_hbm, ao), (log_hbm, logs)]
        )
    ]

    def w_rows(s):
        return wbuf.at[pl.ds(pl.multiple_of(s * shard, 16), shard)]

    own = pltpu.make_async_copy(w_hbm, w_rows(seq), w_recv.at[seq])
    own.start()
    for c in loads:
        c.start()

    barrier = pltpu.get_barrier_semaphore()
    partners = [sibling, far, before, after, side1, side2]
    for d in (1, -1):
        partners += [near(d, 0), near(0, d)]
    for p in partners:
        pl.semaphore_signal(barrier, inc=1, device_id=p, device_id_type=MESH)
    pl.semaphore_wait(barrier, len(partners))

    w_sends = []

    def w_copy(s, device, n):
        return pltpu.make_async_remote_copy(
            w_rows(s), w_rows(s), w_send.at[n], w_recv.at[s],
            device_id=device, device_id_type=MESH,
        )

    def send_w(s, device):
        c = w_copy(s, device, len(w_sends))
        c.start()
        w_sends.append(c)

    def wait_w(s):
        w_copy(s, sibling, 0).wait_recv()

    own.wait()
    send_w(seq, far)
    zf, zg = zhi, 1 - zhi

    def begin(f):
        s = at(f, 0, 0)
        for d in (1, -1):
            send_w(s, near(d, 0))
        for d in (1, -1):
            send_w(s, near(0, d))
        send_w(s, sibling)

    def spread(f, i):
        s = at(f, i, 0)
        for d in (1, -1):
            send_w(s, near(0, d))
        send_w(s, sibling)

    def first_near(f):
        wait_w(at(f, 1, 0))
        wait_w(at(f, -1, 0))
        step = 1 - 2 * f
        send_w(at(f, -step, 0), near(step, 0))
        spread(f, 1)
        spread(f, -1)

    def first_far(f):
        wait_w(at(f, 2, 0))
        spread(f, 2)

    def second_near(f, i):
        for d in (1, -1):
            wait_w(at(f, i, d))
        d = 1 if i in (0, 1) else -1
        send_w(at(f, i, -d), near(0, d))
        for d in (1, -1):
            send_w(at(f, i, d), sibling)

    def second_far(f, i):
        wait_w(at(f, i, 2))
        send_w(at(f, i, 2), sibling)

    def rows_of(b):
        return pl.ds(pl.multiple_of(b * block, 16), block)

    def one_copy(j, b):
        return pltpu.make_async_remote_copy(
            send1.at[j, rows_of(b)], recv1.at[j, rows_of(b)], one_send.at[j, b], one_recv.at[j, b],
            device_id=side1, device_id_type=MESH,
        )

    def two_copy(b):
        return pltpu.make_async_remote_copy(
            send2.at[rows_of(b)], recv2.at[rows_of(b)], two_send.at[b], two_recv.at[b],
            device_id=side2, device_id_type=MESH,
        )

    def do_copy(b):
        return pltpu.make_async_remote_copy(
            do.at[rows_of(b)], do_next.at[rows_of(b)], do_send.at[b], do_rsem.at[b],
            device_id=before, device_id_type=MESH,
        )

    def group(f, d):
        h = lax.rem(y + d + 4, 4)
        for xx in range(4):
            wait_w(slot(h, xx, f, 1 - core))
        mine = lax.rem(h + zlo, 2) == 0

        def product(b):
            rows = pl.ds(pl.multiple_of(h * width + b * block, 16), block)
            return dot(wbuf[rows, :], dl[...], NT)

        @pl.when(mine)
        def _():
            j = jnp.where(h == zlo, 0, 1)

            def body(n, carry):
                b = 2 * n + f
                keep[j, rows_of(b)] = product(b)
                return carry

            lax.fori_loop(0, 4, body, 0)

        @pl.when(jnp.logical_not(mine))
        def _():
            j = jnp.where(h == flip1, 0, 1)

            def body(n, carry):
                b = 2 * n + f
                send1[j, rows_of(b)] = product(b).astype(jnp.bfloat16)
                one_copy(j, b).start()
                return carry

            lax.fori_loop(0, 4, body, 0)

    def combine(f):
        def body(n, carry):
            b = 2 * n + f
            one_copy(1, b).wait_recv()
            both = keep[1, rows_of(b)] + recv1[1, rows_of(b)].astype(jnp.float32)
            send2[rows_of(b)] = both.astype(jnp.bfloat16)
            two_copy(b).start()
            return carry

        lax.fori_loop(0, 4, body, 0)

    def finish(f):
        def body(n, carry):
            b = 2 * n + f
            one_copy(0, b).wait_recv()
            two_copy(b).wait_recv()
            total = keep[0, rows_of(b)] + recv1[0, rows_of(b)].astype(jnp.float32)
            total = total + recv2[rows_of(b)].astype(jnp.float32)
            do[rows_of(b)] = total.astype(jnp.bfloat16)
            do_copy(b).start()
            return carry

        lax.fori_loop(0, 4, body, 0)

    begin(zf)
    first_near(zf)
    first_far(zf)
    second_near(zf, 0)
    second_near(zf, 1)
    wait_w(at(zg, 0, 0))
    begin(zg)
    for c in loads:
        c.wait()
    q_copy = pltpu.make_async_remote_copy(
        q, q_next, q_send.at[0], q_rsem.at[0], device_id=before, device_id_type=MESH
    )
    log_copy = pltpu.make_async_remote_copy(
        logs, log_next, q_send.at[1], q_rsem.at[1], device_id=before, device_id_type=MESH
    )
    q_copy.start()
    log_copy.start()
    second_near(zf, -1)
    second_near(zf, 2)
    second_far(zf, 0)
    group(zf, 0)
    first_near(zg)
    second_far(zf, 1)
    second_far(zf, -1)
    group(zf, 1)
    group(zf, -1)
    first_far(zg)
    second_far(zf, 2)
    group(zf, 2)
    second_near(zg, 0)
    second_near(zg, 1)

    def turn(t, carry):
        c = pl.ds(pl.multiple_of(t * HD, HD), HD)
        ao_t[c, :] = ao[:, c].T
        return carry

    lax.fori_loop(0, width // HD, turn, 0)
    combine(zf)
    second_near(zg, -1)
    second_near(zg, 2)
    second_far(zg, 0)
    group(zg, 0)
    second_far(zg, 1)
    second_far(zg, -1)
    group(zg, 1)
    group(zg, -1)
    finish(zf)
    second_far(zg, 2)
    group(zg, 2)
    combine(zg)
    finish(zg)

    def delta_copy(t):
        return pltpu.make_async_remote_copy(
            delta.at[t], delta_next.at[t], delta_send.at[t], delta_rsem.at[t],
            device_id=before, device_id_type=MESH,
        )

    def back_copy(t):
        return pltpu.make_async_remote_copy(
            dq_send.at[t], dq_recv.at[t], back_send.at[t], back_rsem.at[t],
            device_id=after, device_id_type=MESH,
        )

    def cols(t, n):
        return pl.ds(pl.multiple_of(t * CHUNK + n * HD, HD), HD)

    def row_delta(t, carry):
        for n in range(heads):
            c = cols(t, n)
            prod = do[c, :].astype(jnp.float32) * ao_t[c, :].astype(jnp.float32)
            row = jnp.sum(prod, axis=0, keepdims=True)
            delta[t, n * 4:(n + 1) * 4, :] = jnp.broadcast_to(row, (4, row.shape[1]))
        delta_copy(t).start()
        return carry

    lax.fori_loop(0, chunks, row_delta, 0)

    rows_i = q.shape[0]
    key_at = lax.broadcasted_iota(jnp.int32, (rows_i, rows_i), 0)
    query_at = lax.broadcasted_iota(jnp.int32, (rows_i, rows_i), 1)

    def head_grads(qh, kh, vh, doh, log_row, delta_row, allowed):
        score = dot(kh, qh, NT) * SCALE - log_row
        probs = jnp.exp(jnp.where(allowed, score, MASKED))
        g_value = dot(probs.astype(jnp.bfloat16), doh, NT)
        g_probs = dot(vh, doh, NN)
        low = (probs * (g_probs - delta_row)).astype(jnp.bfloat16)
        g_key = dot(low, qh, NN) * SCALE
        g_query = dot(low, kh, TN) * SCALE
        return g_query, g_key, g_value

    def diagonal(t, carry):
        for n in range(heads):
            c = cols(t, n)
            part = slice(n * HD, (n + 1) * HD)
            g = head_grads(
                q[:, c], k[:, c], v[:, c], do[c, :],
                logs[pl.ds(t * heads + n, 1), :], delta[t, n * 4:n * 4 + 1, :],
                key_at <= query_at,
            )
            dq_acc[t, :, part], dk_acc[t, :, part], dv_acc[t, :, part] = g
        return carry

    lax.fori_loop(0, chunks, diagonal, 0)

    q_copy.wait_recv()
    log_copy.wait_recv()
    limit = jnp.where(seq < 63, rows_i, 0)
    arrived = 0
    for t in range(chunks):
        needed = -(-(t + 1) * CHUNK // block)
        for b in range(arrived, needed):
            do_copy(b).wait_recv()
        arrived = needed
        delta_copy(t).wait_recv()
        for n in range(heads):
            c = slice(t * CHUNK + n * HD, t * CHUNK + (n + 1) * HD)
            part = slice(n * HD, (n + 1) * HD)
            g_query, g_key, g_value = head_grads(
                q_next[:, c], k[:, c], v[:, c], do_next[c, :],
                log_next[t * heads + n:t * heads + n + 1, :], delta_next[t, n * 4:n * 4 + 1, :],
                key_at < limit,
            )
            dq_send[t, :, part] = g_query.astype(jnp.bfloat16)
            dk_ref[:, c] = (dk_acc[t, :, part] + g_key).astype(jnp.bfloat16)
            dv_ref[:, c] = (dv_acc[t, :, part] + g_value).astype(jnp.bfloat16)
        back_copy(t).start()

    def close(t, carry):
        back_copy(t).wait_recv()
        c = pl.ds(pl.multiple_of(t * CHUNK, CHUNK), CHUNK)
        dq_ref[:, c] = (dq_acc[t] + dq_recv[t].astype(jnp.float32)).astype(jnp.bfloat16)
        return carry

    lax.fori_loop(0, chunks, close, 0)

    for c in w_sends:
        c.wait_send()
    q_copy.wait_send()
    log_copy.wait_send()

    def drain_sums(b, carry):
        one_copy(0, b).wait_send()
        one_copy(1, b).wait_send()
        two_copy(b).wait_send()
        do_copy(b).wait_send()
        return carry

    lax.fori_loop(0, width // block, drain_sums, 0)

    def drain(t, carry):
        delta_copy(t).wait_send()
        back_copy(t).wait_send()
        return carry

    lax.fori_loop(0, chunks, drain, 0)


def on_device(query_rows, key_rows, value_rows, attn_out, log_total, d_layer, w_output):
    rows, width = query_rows.shape
    n_heads = log_total.shape[0]
    chunks = width // CHUNK
    seqs = lax.axis_size("seq")
    bf, f32 = jnp.bfloat16, jnp.float32
    full = (rows, width)
    cut = (chunks, rows, CHUNK)
    dma = pltpu.SemaphoreType.DMA
    vm = pltpu.VMEM
    blocks = width // (2 * w_output.shape[0])
    turned = (width, rows)
    scratch = [
        vm((w_output.shape[0] * seqs, width), bf),
        vm(full, bf), vm(full, bf), vm(full, bf), vm(full, bf), vm(full, bf), vm(turned, bf),
        vm((n_heads, rows), f32), vm(full, bf), vm((n_heads, rows), f32),
        vm((2,) + turned, f32), vm((2,) + turned, bf), vm((2,) + turned, bf),
        vm(turned, bf), vm(turned, bf), vm(turned, bf), vm(turned, bf),
        vm((chunks, 8, rows), f32), vm((chunks, 8, rows), f32),
        vm(cut, f32), vm(cut, f32), vm(cut, f32), vm(cut, bf), vm(cut, bf),
        dma((6,)), dma((64,)), dma((64,)), dma((2, blocks)), dma((2, blocks)),
        dma((blocks,)), dma((blocks,)), dma((2,)), dma((2,)),
        dma((blocks,)), dma((blocks,)), dma((chunks,)), dma((chunks,)),
        dma((chunks,)), dma((chunks,)),
    ]
    out = jax.ShapeDtypeStruct(full, bf)
    return pl.pallas_call(
        kernel,
        out_shape=(out, out, out),
        in_specs=[pl.BlockSpec(memory_space=pl.ANY)] * 7,
        out_specs=[pl.BlockSpec(memory_space=pltpu.VMEM)] * 3,
        scratch_shapes=scratch,
        compiler_params=pltpu.CompilerParams(
            collective_id=0, has_side_effects=True, vmem_limit_bytes=56 * 2**20
        ),
    )(query_rows, key_rows, value_rows, attn_out, log_total, d_layer, w_output)


def solution(mesh):
    spec = P("seq", "head")
    return jax.shard_map(
        on_device,
        mesh=mesh,
        in_specs=(spec, spec, spec, spec, P("head", "seq"), spec, spec),
        out_specs=(spec, spec, spec),
        check_vma=False,
    )
```

time: 166 us -> 153 us (0.922)
  the two profiles are of different devices: /device:TPU:10 before, /device:TPU:96 now
where the time goes in v2:
time: 153 us
  Pallas kernels  148 us (97%)
  local copies, waits for them, and re-layouts  4.19 us (3%)
    pallas_call x1, Pallas kernels, on_device(): pl.pallas_call(kernel, out_shape=(out, out, out), in_specs=[pl.BlockSpec(...  148 us
    unnamed x7, local copies, waits for them, and re-layouts  4.19 us

profile of v2, /device:TPU:96, one launch (start us, length us, event | category | flops | bytes accessed | tf_op | source)
XLA Modules:
  0.0 153.1 jit_solution(193714878610360755)
XLA Ops:
  0.6 148.2 %shard_map.94 = (bf16[256,1280]{1,0:T(8,128)(2,1)}, bf16[256,1280]{1,0:T(8,128)(2,1)}, bf16[256,1280]{1,0:T(8,128)(2,1)}) custom-call(bf16[256,1280]{1,0:T(8,128)(2,1)} %q_hbm.1, bf16[256,1280]{1,0:T(8,128)(2,1)} %k_hbm.1, bf16[256,1280]{1,0:T(8,128)(2,1)} %v_hbm.1, bf16[256,1280]{1,0:T(8,128)(2,1)} %ao_hbm.1, f32[10,256]{1,0:T(8,128)} %log_hbm.1, ...), custom_call_target="tpu_custom_call" | custom-call | tf_op jit(solution)/shard_map/pallas_call | solution.py:413
  148.9 0.0 copy-start.1
  148.9 2.0 %copy.13 = bf16[256,1280]{1,0:T(8,128)(2,1)} copy(bf16[256,1280]{1,0:T(8,128)(2,1)} %get-tuple-element.6) | data formatting | bytes 1310720
  150.9 0.0 copy-done.1
  150.9 0.0 copy-start
  150.9 0.8 copy.14
  151.8 0.5 copy-done
  152.2 0.8 copy.15
Async XLA Ops:
  148.9 2.0 %copy-start.1 = (bf16[256,1280]{1,0:T(8,128)(2,1)S(1)}, bf16[256,1280]{1,0:T(8,128)(2,1)}, u32[]{:S(2)}) copy-start(bf16[256,1280]{1,0:T(8,128)(2,1)} %get-tuple-element.7) | copy-start | bytes 1966084
  150.9 1.3 copy-start

commit v3 on v2

v3 whole, which is shorter than its diff:
```python
import functools

import jax
import jax.numpy as jnp
from jax import lax
from jax.experimental import pallas as pl
from jax.experimental.pallas import tpu as pltpu
from jax.sharding import PartitionSpec as P

HD = 128
SCALE = HD ** (-0.5)
MASKED = -1e30
CHUNK = 256
MESH = pl.DeviceIdType.MESH
NT = (((1,), (1,)), ((), ()))
NN = (((1,), (0,)), ((), ()))
TN = (((0,), (0,)), ((), ()))


def dot(a, b, dims):
    return lax.dot_general(a, b, dims, preferred_element_type=jnp.float32)


def kernel(
    q_hbm, k_hbm, v_hbm, ao_hbm, log_hbm, dl_hbm, w_hbm,
    dq_ref, dk_ref, dv_ref,
    wbuf, dl, q, k, v, ao, ao_t, logs, q_next, log_next,
    keep, send1, recv1, send2, do, do_parts, do_next, next_parts, delta, delta_next,
    dq_acc, dk_acc, dv_acc, dq_send, dq_recv,
    local_sem, w_send, w_recv, dl_sem, one_send, one_recv, two_send, two_recv,
    q_send, q_rsem, do_send, do_rsem, delta_send, delta_rsem, back_send, back_rsem,
):
    seq = lax.axis_index("seq")
    zlo = lax.axis_index("head")
    core = lax.rem(seq, 2)
    zhi = lax.rem(seq // 2, 2)
    x = lax.rem(seq // 4, 4)
    y = seq // 16
    shard = w_hbm.shape[0]
    part = 4 * shard
    width = q.shape[1]
    chunks = width // CHUNK
    heads = CHUNK // HD

    def device(yy, xx, hh, cc):
        return ((lax.rem(yy + 4, 4) * 4 + lax.rem(xx + 4, 4)) * 2 + hh) * 2 + cc

    flip1 = zlo + 1 - 2 * lax.rem(zlo, 2)
    flip2 = lax.rem(zlo + 2, 4)
    sibling = (device(y, x, zhi, 1 - core), zlo)
    far = (device(y, x, 1 - zhi, core), zlo)
    cross1 = (device(y, x, zhi, 1 - core), flip1)
    cross2 = (device(y, x, 1 - zhi, 1 - core), flip1)
    before = (lax.rem(seq + 63, 64), zlo)
    after = (lax.rem(seq + 1, 64), zlo)
    side1 = (seq, flip1)
    side2 = (seq, flip2)

    pair = zlo // 2
    half = lax.rem(zlo, 2)
    home = core == half

    def slot(yy, c, f, xx):
        return ((lax.rem(yy + 4, 4) * 2 + c) * 2 + f) * 4 + lax.rem(xx + 4, 4)

    def place(i, j):
        return y + core * i + (1 - core) * j, x + (1 - core) * i + core * j

    def at(f, i, j):
        yy, xx = place(i, j)
        return slot(yy, core, f, xx)

    def near(i, j):
        yy, xx = place(i, j)
        return (device(yy, xx, zhi, core), zlo)

    loads = [
        pltpu.make_async_copy(src, dst, local_sem.at[n])
        for n, (src, dst) in enumerate(
            [(dl_hbm, dl.at[half]), (q_hbm, q), (k_hbm, k), (v_hbm, v), (ao_hbm, ao), (log_hbm, logs)]
        )
    ]

    def w_rows(s):
        return wbuf.at[pl.ds(pl.multiple_of(s * shard, 16), shard)]

    own_slot = slot(y, half, zhi, x)

    @pl.when(home)
    def _():
        pltpu.make_async_copy(w_hbm, w_rows(own_slot), w_recv.at[own_slot]).start()

    for c in loads:
        c.start()

    barrier = pltpu.get_barrier_semaphore()
    partners = [sibling, far, cross1, cross2, before, after, side1, side2]
    for d in (1, -1):
        partners += [near(d, 0), near(0, d)]
    for p in partners:
        pl.semaphore_signal(barrier, inc=1, device_id=p, device_id_type=MESH)
    pl.semaphore_wait(barrier, len(partners))

    w_sends = []

    def w_copy(s, device, n):
        return pltpu.make_async_remote_copy(
            w_rows(s), w_rows(s), w_send.at[n], w_recv.at[s],
            device_id=device, device_id_type=MESH,
        )

    def send_w(s, device):
        c = w_copy(s, device, len(w_sends))
        c.start()
        w_sends.append(c)

    def wait_w(s):
        w_copy(s, sibling, 0).wait_recv()

    def z_move(n, device):
        return pltpu.make_async_remote_copy(
            w_hbm, w_rows(own_slot), w_send.at[n], w_recv.at[own_slot],
            device_id=device, device_id_type=MESH,
        )

    @pl.when(home)
    def _():
        z_move(62, far).start()

    @pl.when(jnp.logical_not(home))
    def _():
        z_move(62, cross1).start()
        z_move(63, cross2).start()

    zf, zg = zhi, 1 - zhi

    def begin(f):
        s = at(f, 0, 0)
        for d in (1, -1):
            send_w(s, near(d, 0))
        for d in (1, -1):
            send_w(s, near(0, d))
        send_w(s, sibling)

    def spread(f, i):
        s = at(f, i, 0)
        for d in (1, -1):
            send_w(s, near(0, d))
        send_w(s, sibling)

    def first_near(f):
        wait_w(at(f, 1, 0))
        wait_w(at(f, -1, 0))
        step = 1 - 2 * f
        send_w(at(f, -step, 0), near(step, 0))
        spread(f, 1)
        spread(f, -1)

    def first_far(f):
        wait_w(at(f, 2, 0))
        spread(f, 2)

    def second_near(f, i):
        for d in (1, -1):
            wait_w(at(f, i, d))
        d = 1 if i in (0, 1) else -1
        send_w(at(f, i, -d), near(0, d))
        for d in (1, -1):
            send_w(at(f, i, d), sibling)

    def second_far(f, i):
        wait_w(at(f, i, 2))
        send_w(at(f, i, 2), sibling)

    def one_copy(j, f):
        return pltpu.make_async_remote_copy(
            send1.at[j, f], recv1.at[j, f], one_send.at[j, f], one_recv.at[j, f],
            device_id=side2, device_id_type=MESH,
        )

    def two_copy(f):
        return pltpu.make_async_remote_copy(
            send2.at[f], do_parts.at[half, f], two_send.at[f], two_recv.at[f],
            device_id=side1, device_id_type=MESH,
        )

    def two_arrival(f):
        return pltpu.make_async_remote_copy(
            send2.at[f], do_parts.at[1 - half, f], two_send.at[f], two_recv.at[f],
            device_id=side1, device_id_type=MESH,
        )

    def do_copy(b, f):
        return pltpu.make_async_remote_copy(
            do_parts.at[b, f], next_parts.at[b, f], do_send.at[b, f], do_rsem.at[b, f],
            device_id=before, device_id_type=MESH,
        )

    def group(f, d):
        h = lax.rem(y + d + 4, 4)
        for xx in range(4):
            wait_w(slot(h, 1 - core, f, xx))
        mine = h // 2 == pair
        j = lax.rem(h, 2)

        def product():
            total = 0.0
            for c in range(2):
                rows = pl.ds(pl.multiple_of(slot(h, c, f, 0) * shard, 16), part)
                total += dot(wbuf[rows, :], dl[c], NT)
            return total

        @pl.when(mine)
        def _():
            keep[j, f] = product()

        @pl.when(jnp.logical_not(mine))
        def _():
            send1[j, f] = product().astype(jnp.bfloat16)
            one_copy(j, f).start()

    def combine(f, d):
        h = lax.rem(y + d + 4, 4)
        j = lax.rem(h, 2)

        def total():
            one_copy(j, f).wait_recv()
            return (keep[j, f] + recv1[j, f].astype(jnp.float32)).astype(jnp.bfloat16)

        @pl.when(h == zlo)
        def _():
            do_parts[half, f] = total()
            do_copy(half, f).start()

        @pl.when(h == flip1)
        def _():
            send2[f] = total()
            two_copy(f).start()

    def forward(f, d):
        h = lax.rem(y + d + 4, 4)

        @pl.when(h == zlo)
        def _():
            two_arrival(f).wait_recv()
            do_copy(1 - half, f).start()

    def arrange(parts, whole):
        for m in range(16):
            xx, f, b = m // 4, m // 2 % 2, m % 2
            whole[m * shard:(m + 1) * shard, :] = parts[b, f, xx * shard:(xx + 1) * shard, :]

    wait_w(at(zf, 0, 0))
    begin(zf)
    first_near(zf)
    dl_copy = pltpu.make_async_remote_copy(
        dl_hbm, dl.at[half], dl_sem.at[0], dl_sem.at[1], device_id=side1, device_id_type=MESH
    )
    dl_arrival = pltpu.make_async_remote_copy(
        dl_hbm, dl.at[1 - half], dl_sem.at[0], dl_sem.at[1], device_id=side1, device_id_type=MESH
    )
    dl_copy.start()
    first_far(zf)
    second_near(zf, 0)
    second_near(zf, 1)
    wait_w(at(zg, 0, 0))
    begin(zg)
    for c in loads:
        c.wait()
    q_copy = pltpu.make_async_remote_copy(
        q, q_next, q_send.at[0], q_rsem.at[0], device_id=before, device_id_type=MESH
    )
    log_copy = pltpu.make_async_remote_copy(
        logs, log_next, q_send.at[1], q_rsem.at[1], device_id=before, device_id_type=MESH
    )
    q_copy.start()
    log_copy.start()
    second_near(zf, -1)
    second_near(zf, 2)
    second_far(zf, 0)
    first_near(zg)
    dl_arrival.wait_recv()
    group(zf, 0)
    second_far(zf, 1)
    second_far(zf, -1)
    group(zf, 1)
    group(zf, -1)
    first_far(zg)
    second_far(zf, 2)
    group(zf, 2)
    second_near(zg, 0)
    second_near(zg, 1)
    combine(zf, 0)
    combine(zf, 1)

    def turn(t, carry):
        c = pl.ds(pl.multiple_of(t * HD, HD), HD)
        ao_t[c, :] = ao[:, c].T
        return carry

    lax.fori_loop(0, width // HD, turn, 0)
    second_near(zg, -1)
    second_near(zg, 2)
    combine(zf, -1)
    combine(zf, 2)
    second_far(zg, 0)
    group(zg, 0)
    forward(zf, 0)
    forward(zf, 1)
    second_far(zg, 1)
    second_far(zg, -1)
    group(zg, 1)
    group(zg, -1)
    forward(zf, -1)
    forward(zf, 2)
    combine(zg, 0)
    second_far(zg, 2)
    group(zg, 2)
    combine(zg, 1)
    combine(zg, -1)
    forward(zg, 0)
    forward(zg, 1)
    combine(zg, 2)
    forward(zg, -1)
    forward(zg, 2)
    arrange(do_parts, do)

    def delta_copy(t):
        return pltpu.make_async_remote_copy(
            delta.at[t], delta_next.at[t], delta_send.at[t], delta_rsem.at[t],
            device_id=before, device_id_type=MESH,
        )

    def back_copy(t):
        return pltpu.make_async_remote_copy(
            dq_send.at[t], dq_recv.at[t], back_send.at[t], back_rsem.at[t],
            device_id=after, device_id_type=MESH,
        )

    def cols(t, n):
        return pl.ds(pl.multiple_of(t * CHUNK + n * HD, HD), HD)

    def row_delta(t, carry):
        for n in range(heads):
            c = cols(t, n)
            prod = do[c, :].astype(jnp.float32) * ao_t[c, :].astype(jnp.float32)
            row = jnp.sum(prod, axis=0, keepdims=True)
            delta[t, n * 4:(n + 1) * 4, :] = jnp.broadcast_to(row, (4, row.shape[1]))
        delta_copy(t).start()
        return carry

    lax.fori_loop(0, chunks, row_delta, 0)

    rows_i = q.shape[0]
    key_at = lax.broadcasted_iota(jnp.int32, (rows_i, rows_i), 0)
    query_at = lax.broadcasted_iota(jnp.int32, (rows_i, rows_i), 1)

    def head_grads(qh, kh, vh, doh, log_row, delta_row, allowed):
        score = dot(kh, qh, NT) * SCALE - log_row
        probs = jnp.exp(jnp.where(allowed, score, MASKED))
        g_value = dot(probs.astype(jnp.bfloat16), doh, NT)
        g_probs = dot(vh, doh, NN)
        low = (probs * (g_probs - delta_row)).astype(jnp.bfloat16)
        g_key = dot(low, qh, NN) * SCALE
        g_query = dot(low, kh, TN) * SCALE
        return g_query, g_key, g_value

    for t in range(chunks):
        for n in range(heads):
            c = slice(t * CHUNK + n * HD, t * CHUNK + (n + 1) * HD)
            own = slice(n * HD, (n + 1) * HD)
            g = head_grads(
                q[:, c], k[:, c], v[:, c], do[c, :],
                logs[t * heads + n:t * heads + n + 1, :], delta[t, n * 4:n * 4 + 1, :],
                key_at <= query_at,
            )
            dq_acc[t, :, own], dk_acc[t, :, own], dv_acc[t, :, own] = g

    q_copy.wait_recv()
    log_copy.wait_recv()
    limit = jnp.where(seq < 63, rows_i, 0)
    for b in range(2):
        for f in range(2):
            do_copy(b, f).wait_recv()
    arrange(next_parts, do_next)
    for t in range(chunks):
        delta_copy(t).wait_recv()
        for n in range(heads):
            c = slice(t * CHUNK + n * HD, t * CHUNK + (n + 1) * HD)
            own = slice(n * HD, (n + 1) * HD)
            g_query, g_key, g_value = head_grads(
                q_next[:, c], k[:, c], v[:, c], do_next[c, :],
                log_next[t * heads + n:t * heads + n + 1, :], delta_next[t, n * 4:n * 4 + 1, :],
                key_at < limit,
            )
            dq_send[t, :, own] = g_query.astype(jnp.bfloat16)
            dk_ref[:, c] = (dk_acc[t, :, own] + g_key).astype(jnp.bfloat16)
            dv_ref[:, c] = (dv_acc[t, :, own] + g_value).astype(jnp.bfloat16)
        back_copy(t).start()

    def close(t, carry):
        back_copy(t).wait_recv()
        c = pl.ds(pl.multiple_of(t * CHUNK, CHUNK), CHUNK)
        dq_ref[:, c] = (dq_acc[t] + dq_recv[t].astype(jnp.float32)).astype(jnp.bfloat16)
        return carry

    lax.fori_loop(0, chunks, close, 0)

    for c in w_sends:
        c.wait_send()
    z_move(62, far).wait_send()

    @pl.when(jnp.logical_not(home))
    def _():
        z_move(63, cross2).wait_send()

    dl_copy.wait_send()
    q_copy.wait_send()
    log_copy.wait_send()

    for b in range(2):
        two_copy(b).wait_send()
        for f in range(2):
            one_copy(b, f).wait_send()
            do_copy(b, f).wait_send()

    def drain(t, carry):
        delta_copy(t).wait_send()
        back_copy(t).wait_send()
        return carry

    lax.fori_loop(0, chunks, drain, 0)


def on_device(query_rows, key_rows, value_rows, attn_out, log_total, d_layer, w_output):
    rows, width = query_rows.shape
    n_heads = log_total.shape[0]
    chunks = width // CHUNK
    seqs = lax.axis_size("seq")
    bf, f32 = jnp.bfloat16, jnp.float32
    full = (rows, width)
    cut = (chunks, rows, CHUNK)
    dma = pltpu.SemaphoreType.DMA
    vm = pltpu.VMEM
    part = 4 * w_output.shape[0]
    turned = (width, rows)
    scratch = [
        vm((w_output.shape[0] * seqs, width), bf),
        vm((2,) + full, bf), vm(full, bf), vm(full, bf), vm(full, bf), vm(full, bf), vm(turned, bf),
        vm((n_heads, rows), f32), vm(full, bf), vm((n_heads, rows), f32),
        vm((2, 2, part, rows), f32), vm((2, 2, part, rows), bf), vm((2, 2, part, rows), bf),
        vm((2, part, rows), bf), vm(turned, bf), vm((2, 2, part, rows), bf),
        vm(turned, bf), vm((2, 2, part, rows), bf),
        vm((chunks, 8, rows), f32), vm((chunks, 8, rows), f32),
        vm(cut, f32), vm(cut, f32), vm(cut, f32), vm(cut, bf), vm(cut, bf),
        dma((6,)), dma((64,)), dma((64,)), dma((2,)), dma((2, 2)), dma((2, 2)),
        dma((2,)), dma((2,)), dma((2,)), dma((2,)),
        dma((2, 2)), dma((2, 2)), dma((chunks,)), dma((chunks,)),
        dma((chunks,)), dma((chunks,)),
    ]
    out = jax.ShapeDtypeStruct(full, bf)
    return pl.pallas_call(
        kernel,
        out_shape=(out, out, out),
        in_specs=[pl.BlockSpec(memory_space=pl.ANY)] * 7,
        out_specs=[pl.BlockSpec(memory_space=pltpu.VMEM)] * 3,
        scratch_shapes=scratch,
        compiler_params=pltpu.CompilerParams(
            collective_id=0, has_side_effects=True, vmem_limit_bytes=56 * 2**20
        ),
    )(query_rows, key_rows, value_rows, attn_out, log_total, d_layer, w_output)


def solution(mesh):
    spec = P("seq", "head")
    return jax.shard_map(
        on_device,
        mesh=mesh,
        in_specs=(spec, spec, spec, spec, P("head", "seq"), spec, spec),
        out_specs=(spec, spec, spec),
        check_vma=False,
    )
```

time: 153 us -> 138 us (0.902)
  the two profiles are of different devices: /device:TPU:96 before, /device:TPU:56 now
where the time goes in v3:
time: 138 us
  Pallas kernels  133 us (96%)
  local copies, waits for them, and re-layouts  4.19 us (3%)
    pallas_call x1, Pallas kernels, on_device(): pl.pallas_call(kernel, out_shape=(out, out, out), in_specs=[pl.BlockSpec(...  133 us
    unnamed x7, local copies, waits for them, and re-layouts  4.19 us

profile of v3, /device:TPU:56, one launch (start us, length us, event | category | flops | bytes accessed | tf_op | source)
XLA Modules:
  0.0 138.0 jit_solution(2112295367530297019)
XLA Ops:
  0.6 133.1 %shard_map.94 = (bf16[256,1280]{1,0:T(8,128)(2,1)}, bf16[256,1280]{1,0:T(8,128)(2,1)}, bf16[256,1280]{1,0:T(8,128)(2,1)}) custom-call(bf16[256,1280]{1,0:T(8,128)(2,1)} %q_hbm.1, bf16[256,1280]{1,0:T(8,128)(2,1)} %k_hbm.1, bf16[256,1280]{1,0:T(8,128)(2,1)} %v_hbm.1, bf16[256,1280]{1,0:T(8,128)(2,1)} %ao_hbm.1, f32[10,256]{1,0:T(8,128)} %log_hbm.1, ...), custom_call_target="tpu_custom_call" | custom-call | tf_op jit(solution)/shard_map/pallas_call | solution.py:462
  133.8 0.0 copy-start.1
  133.8 2.0 %copy.13 = bf16[256,1280]{1,0:T(8,128)(2,1)} copy(bf16[256,1280]{1,0:T(8,128)(2,1)} %get-tuple-element.6) | data formatting | bytes 1310720
  135.8 0.0 copy-done.1
  135.8 0.0 copy-start
  135.8 0.8 copy.14
  136.6 0.5 copy-done
  137.1 0.8 copy.15
Async XLA Ops:
  133.8 2.0 %copy-start.1 = (bf16[256,1280]{1,0:T(8,128)(2,1)S(1)}, bf16[256,1280]{1,0:T(8,128)(2,1)}, u32[]{:S(2)}) copy-start(bf16[256,1280]{1,0:T(8,128)(2,1)} %get-tuple-element.7) | copy-start | bytes 1966084
  135.8 1.3 copy-start

commit v4 on v3

--- a/solution.py
+++ b/solution.py
@@ -27,7 +27,7 @@
     wbuf, dl, q, k, v, ao, ao_t, logs, q_next, log_next,
     keep, send1, recv1, send2, do, do_parts, do_next, next_parts, delta, delta_next,
     dq_acc, dk_acc, dv_acc, dq_send, dq_recv,
-    local_sem, w_send, w_recv, dl_sem, one_send, one_recv, two_send, two_recv,
+    local_sem, w_send, w_recv, dl_sem, one_send, one_recv, two_send, two_recv, side_send,
     q_send, q_rsem, do_send, do_rsem, delta_send, delta_rsem, back_send, back_rsem,
 ):
     seq = lax.axis_index("seq")
@@ -55,6 +55,8 @@
     after = (lax.rem(seq + 1, 64), zlo)
     side1 = (seq, flip1)
     side2 = (seq, flip2)
+    before1 = (lax.rem(seq + 63, 64), flip1)
+    after1 = (lax.rem(seq + 1, 64), flip1)
 
     pair = zlo // 2
     half = lax.rem(zlo, 2)
@@ -94,9 +96,10 @@
         c.start()
 
     barrier = pltpu.get_barrier_semaphore()
-    partners = [sibling, far, cross1, cross2, before, after, side1, side2]
+    partners = [sibling, far, cross1, cross2, before, after, before1, after1, side1, side2]
     for d in (1, -1):
         partners += [near(d, 0), near(0, d)]
+    partners += [near(2, 0)]
     for p in partners:
         pl.semaphore_signal(barrier, inc=1, device_id=p, device_id_type=MESH)
     pl.semaphore_wait(barrier, len(partners))
@@ -136,7 +139,7 @@
 
     def begin(f):
         s = at(f, 0, 0)
-        for d in (1, -1):
+        for d in (1, -1, 2):
             send_w(s, near(d, 0))
         for d in (1, -1):
             send_w(s, near(0, d))
@@ -151,8 +154,6 @@
     def first_near(f):
         wait_w(at(f, 1, 0))
         wait_w(at(f, -1, 0))
-        step = 1 - 2 * f
-        send_w(at(f, -step, 0), near(step, 0))
         spread(f, 1)
         spread(f, -1)
 
@@ -192,8 +193,14 @@
 
     def do_copy(b, f):
         return pltpu.make_async_remote_copy(
-            do_parts.at[b, f], next_parts.at[b, f], do_send.at[b, f], do_rsem.at[b, f],
+            do_parts.at[b, f], next_parts.at[b, f], do_send.at[f], do_rsem.at[b, f],
             device_id=before, device_id_type=MESH,
+        )
+
+    def side_copy(f):
+        return pltpu.make_async_remote_copy(
+            send2.at[f], next_parts.at[half, f], side_send.at[f], do_rsem.at[half, f],
+            device_id=before1, device_id_type=MESH,
         )
 
     def group(f, d):
@@ -236,23 +243,14 @@
         def _():
             send2[f] = total()
             two_copy(f).start()
-
-    def forward(f, d):
-        h = lax.rem(y + d + 4, 4)
-
-        @pl.when(h == zlo)
-        def _():
-            two_arrival(f).wait_recv()
-            do_copy(1 - half, f).start()
+            side_copy(f).start()
 
     def arrange(parts, whole):
         for m in range(16):
             xx, f, b = m // 4, m // 2 % 2, m % 2
             whole[m * shard:(m + 1) * shard, :] = parts[b, f, xx * shard:(xx + 1) * shard, :]
 
-    wait_w(at(zf, 0, 0))
-    begin(zf)
-    first_near(zf)
+    e = 2 * lax.rem(y, 2) - 1
     dl_copy = pltpu.make_async_remote_copy(
         dl_hbm, dl.at[half], dl_sem.at[0], dl_sem.at[1], device_id=side1, device_id_type=MESH
     )
@@ -260,6 +258,9 @@
         dl_hbm, dl.at[1 - half], dl_sem.at[0], dl_sem.at[1], device_id=side1, device_id_type=MESH
     )
     dl_copy.start()
+    wait_w(at(zf, 0, 0))
+    begin(zf)
+    first_near(zf)
     first_far(zf)
     second_near(zf, 0)
     second_near(zf, 1)
@@ -283,46 +284,39 @@
     group(zf, 0)
     second_far(zf, 1)
     second_far(zf, -1)
-    group(zf, 1)
-    group(zf, -1)
+    group(zf, e)
+    group(zf, -e)
     first_far(zg)
     second_far(zf, 2)
     group(zf, 2)
-    second_near(zg, 0)
-    second_near(zg, 1)
-    combine(zf, 0)
-    combine(zf, 1)
-
     def turn(t, carry):
         c = pl.ds(pl.multiple_of(t * HD, HD), HD)
         ao_t[c, :] = ao[:, c].T
         return carry
 
     lax.fori_loop(0, width // HD, turn, 0)
+    second_near(zg, 0)
+    second_near(zg, 1)
+    combine(zf, 0)
+    combine(zf, e)
     second_near(zg, -1)
-    second_near(zg, 2)
-    combine(zf, -1)
-    combine(zf, 2)
     second_far(zg, 0)
     group(zg, 0)
-    forward(zf, 0)
-    forward(zf, 1)
+    second_near(zg, 2)
+    combine(zf, -e)
+    combine(zf, 2)
     second_far(zg, 1)
     second_far(zg, -1)
-    group(zg, 1)
-    group(zg, -1)
-    forward(zf, -1)
-    forward(zf, 2)
+    group(zg, e)
+    group(zg, -e)
     combine(zg, 0)
+    combine(zg, e)
     second_far(zg, 2)
     group(zg, 2)
-    combine(zg, 1)
-    combine(zg, -1)
-    forward(zg, 0)
-    forward(zg, 1)
+    combine(zg, -e)
     combine(zg, 2)
-    forward(zg, -1)
-    forward(zg, 2)
+    for f in range(2):
+        two_arrival(f).wait_recv()
     arrange(do_parts, do)
 
     def delta_copy(t):
@@ -420,9 +414,10 @@
 
     for b in range(2):
         two_copy(b).wait_send()
+        side_copy(b).wait_send()
+        do_copy(half, b).wait_send()
         for f in range(2):
             one_copy(b, f).wait_send()
-            do_copy(b, f).wait_send()
 
     def drain(t, carry):
         delta_copy(t).wait_send()
@@ -454,8 +449,8 @@
         vm((chunks, 8, rows), f32), vm((chunks, 8, rows), f32),
         vm(cut, f32), vm(cut, f32), vm(cut, f32), vm(cut, bf), vm(cut, bf),
         dma((6,)), dma((64,)), dma((64,)), dma((2,)), dma((2, 2)), dma((2, 2)),
-        dma((2,)), dma((2,)), dma((2,)), dma((2,)),
-        dma((2, 2)), dma((2, 2)), dma((chunks,)), dma((chunks,)),
+        dma((2,)), dma((2,)), dma((2,)), dma((2,)), dma((2,)),
+        dma((2,)), dma((2, 2)), dma((chunks,)), dma((chunks,)),
         dma((chunks,)), dma((chunks,)),
     ]
     out = jax.ShapeDtypeStruct(full, bf)

time: 138 us -> 130 us (0.942)
  the two profiles are of different devices: /device:TPU:56 before, /device:TPU:32 now
where the time goes in v4:
time: 130 us; the launch traced here: 128 us
  Pallas kernels  123 us (95%)
  local copies, waits for them, and re-layouts  4.19 us (3%)
    pallas_call x1, Pallas kernels, on_device(): pl.pallas_call(kernel, out_shape=(out, out, out), in_specs=[pl.BlockSpec(...  123 us
    unnamed x7, local copies, waits for them, and re-layouts  4.19 us

profile of v4, /device:TPU:32, one launch (start us, length us, event | category | flops | bytes accessed | tf_op | source)
XLA Modules:
  0.0 127.8 jit_solution(16450270475177354938)
XLA Ops:
  0.6 122.9 %shard_map.94 = (bf16[256,1280]{1,0:T(8,128)(2,1)}, bf16[256,1280]{1,0:T(8,128)(2,1)}, bf16[256,1280]{1,0:T(8,128)(2,1)}) custom-call(bf16[256,1280]{1,0:T(8,128)(2,1)} %q_hbm.1, bf16[256,1280]{1,0:T(8,128)(2,1)} %k_hbm.1, bf16[256,1280]{1,0:T(8,128)(2,1)} %v_hbm.1, bf16[256,1280]{1,0:T(8,128)(2,1)} %ao_hbm.1, f32[10,256]{1,0:T(8,128)} %log_hbm.1, ...), custom_call_target="tpu_custom_call" | custom-call | tf_op jit(solution)/shard_map/pallas_call | solution.py:457
  123.5 0.0 copy-start.1
  123.6 2.0 %copy.13 = bf16[256,1280]{1,0:T(8,128)(2,1)} copy(bf16[256,1280]{1,0:T(8,128)(2,1)} %get-tuple-element.6) | data formatting | bytes 1310720
  125.6 0.0 copy-done.1
  125.6 0.0 copy-start
  125.6 0.8 copy.14
  126.4 0.5 copy-done
  126.9 0.8 copy.15
Async XLA Ops:
  123.5 2.0 %copy-start.1 = (bf16[256,1280]{1,0:T(8,128)(2,1)S(1)}, bf16[256,1280]{1,0:T(8,128)(2,1)}, u32[]{:S(2)}) copy-start(bf16[256,1280]{1,0:T(8,128)(2,1)} %get-tuple-element.7) | copy-start | bytes 1966084
  125.6 1.3 %copy-start = (bf16[256,1280]{1,0:T(8,128)(2,1)S(1)}, bf16[256,1280]{1,0:T(8,128)(2,1)}, u32[]{:S(2)}) copy-start(bf16[256,1280]{1,0:T(8,128)(2,1)} %get-tuple-element.8) | copy-start | bytes 1966084

commit v5 on v4

--- a/solution.py
+++ b/solution.py
@@ -23,12 +23,12 @@
 
 def kernel(
     q_hbm, k_hbm, v_hbm, ao_hbm, log_hbm, dl_hbm, w_hbm,
-    dq_ref, dk_ref, dv_ref,
+    dq_hbm, dk_hbm, dv_hbm,
     wbuf, dl, q, k, v, ao, ao_t, logs, q_next, log_next,
     keep, send1, recv1, send2, do, do_parts, do_next, next_parts, delta, delta_next,
-    dq_acc, dk_acc, dv_acc, dq_send, dq_recv,
+    dq_acc, dk_acc, dv_acc, dq_send, dq_recv, dq_ref, dk_ref, dv_ref,
     local_sem, w_send, w_recv, dl_sem, one_send, one_recv, two_send, two_recv, side_send,
-    q_send, q_rsem, do_send, do_rsem, delta_send, delta_rsem, back_send, back_rsem,
+    q_send, q_rsem, do_send, do_rsem, delta_send, delta_rsem, back_send, back_rsem, out_sem,
 ):
     seq = lax.axis_index("seq")
     zlo = lax.axis_index("head")
@@ -331,6 +331,11 @@
             device_id=after, device_id_type=MESH,
         )
 
+    def out_copy(n, t):
+        src, dst = ((dq_ref, dq_hbm), (dk_ref, dk_hbm), (dv_ref, dv_hbm))[n]
+        c = pl.ds(t * CHUNK, CHUNK)
+        return pltpu.make_async_copy(src.at[:, c], dst.at[:, c], out_sem.at[n, t])
+
     def cols(t, n):
         return pl.ds(pl.multiple_of(t * CHUNK + n * HD, HD), HD)
 
@@ -391,17 +396,17 @@
             dk_ref[:, c] = (dk_acc[t, :, own] + g_key).astype(jnp.bfloat16)
             dv_ref[:, c] = (dv_acc[t, :, own] + g_value).astype(jnp.bfloat16)
         back_copy(t).start()
-
-    def close(t, carry):
-        back_copy(t).wait_recv()
-        c = pl.ds(pl.multiple_of(t * CHUNK, CHUNK), CHUNK)
-        dq_ref[:, c] = (dq_acc[t] + dq_recv[t].astype(jnp.float32)).astype(jnp.bfloat16)
-        return carry
-
-    lax.fori_loop(0, chunks, close, 0)
+        out_copy(1, t).start()
+        out_copy(2, t).start()
 
     for c in w_sends:
         c.wait_send()
+    for t in range(chunks):
+        back_copy(t).wait_recv()
+        c = slice(t * CHUNK, (t + 1) * CHUNK)
+        dq_ref[:, c] = (dq_acc[t] + dq_recv[t].astype(jnp.float32)).astype(jnp.bfloat16)
+        out_copy(0, t).start()
+
     z_move(62, far).wait_send()
 
     @pl.when(jnp.logical_not(home))
@@ -425,6 +430,22 @@
         return carry
 
     lax.fori_loop(0, chunks, drain, 0)
+    for n in range(3):
+        for t in range(chunks):
+            out_copy(n, t).wait()
+
+
+def hand_over(a, b, c, x, y, z, hold, sem):
+    pairs = [(a, x), (b, y), (c, z)]
+    arrive = [pltpu.make_async_copy(src, hold.at[n], sem.at[0, n]) for n, (src, dst) in enumerate(pairs)]
+    leave = [pltpu.make_async_copy(hold.at[n], dst, sem.at[1, n]) for n, (src, dst) in enumerate(pairs)]
+    for copy in arrive:
+        copy.start()
+    for n in range(3):
+        arrive[n].wait()
+        leave[n].start()
+    for copy in leave:
+        copy.wait()
 
 
 def on_device(query_rows, key_rows, value_rows, attn_out, log_total, d_layer, w_output):
@@ -448,22 +469,30 @@
         vm(turned, bf), vm((2, 2, part, rows), bf),
         vm((chunks, 8, rows), f32), vm((chunks, 8, rows), f32),
         vm(cut, f32), vm(cut, f32), vm(cut, f32), vm(cut, bf), vm(cut, bf),
+        vm(full, bf), vm(full, bf), vm(full, bf),
         dma((6,)), dma((64,)), dma((64,)), dma((2,)), dma((2, 2)), dma((2, 2)),
         dma((2,)), dma((2,)), dma((2,)), dma((2,)), dma((2,)),
         dma((2,)), dma((2, 2)), dma((chunks,)), dma((chunks,)),
-        dma((chunks,)), dma((chunks,)),
+        dma((chunks,)), dma((chunks,)), dma((3, chunks)),
     ]
     out = jax.ShapeDtypeStruct(full, bf)
-    return pl.pallas_call(
+    grads = pl.pallas_call(
         kernel,
         out_shape=(out, out, out),
         in_specs=[pl.BlockSpec(memory_space=pl.ANY)] * 7,
-        out_specs=[pl.BlockSpec(memory_space=pltpu.VMEM)] * 3,
+        out_specs=[pl.BlockSpec(memory_space=pl.ANY)] * 3,
         scratch_shapes=scratch,
         compiler_params=pltpu.CompilerParams(
             collective_id=0, has_side_effects=True, vmem_limit_bytes=56 * 2**20
         ),
     )(query_rows, key_rows, value_rows, attn_out, log_total, d_layer, w_output)
+    return pl.pallas_call(
+        hand_over,
+        out_shape=(out, out, out),
+        in_specs=[pl.BlockSpec(memory_space=pl.ANY)] * 3,
+        out_specs=[pl.BlockSpec(memory_space=pl.ANY)] * 3,
+        scratch_shapes=[vm((3,) + full, bf), dma((2, 3))],
+    )(*grads)
 
 
 def solution(mesh):

time: 130 us -> 128 us (0.985)
  local copies, waits for them, and re-layouts: 4.19 us -> 0 us
  Pallas kernels: 123 us -> 125 us
    unnamed x7 -> x0, local copies, waits for them, and re-layouts: 4.19 us -> none
    pallas_call x0 -> x1, Pallas kernels: none -> 2.41 us  [on_device(): pl.pallas_call(hand_over, out_shape=(out, out, out), in_specs=[pl.BlockSp...]
where the time goes in v5:
time: 128 us; the launch traced here: 126 us
  Pallas kernels  125 us (98%)
    pallas_call x1, Pallas kernels, on_device(): pl.pallas_call(kernel, out_shape=(out, out, out), in_specs=[pl.BlockSpec(...  122 us

profile of v5, /device:TPU:32, one launch (start us, length us, event | category | flops | bytes accessed | tf_op | source)
XLA Modules:
  0.0 125.5 jit_solution(17078090799957083553)
XLA Ops:
  0.6 122.3 %shard_map.94 = (bf16[256,1280]{1,0:T(8,128)(2,1)}, bf16[256,1280]{1,0:T(8,128)(2,1)}, bf16[256,1280]{1,0:T(8,128)(2,1)}) custom-call(bf16[256,1280]{1,0:T(8,128)(2,1)} %q_hbm.1, bf16[256,1280]{1,0:T(8,128)(2,1)} %k_hbm.1, bf16[256,1280]{1,0:T(8,128)(2,1)} %v_hbm.1, bf16[256,1280]{1,0:T(8,128)(2,1)} %ao_hbm.1, f32[10,256]{1,0:T(8,128)} %log_hbm.1, ...), custom_call_target="tpu_custom_call" | custom-call | tf_op jit(solution)/shard_map/pallas_call | solution.py:479
  123.0 2.4 %shard_map.95 = (bf16[256,1280]{1,0:T(8,128)(2,1)}, bf16[256,1280]{1,0:T(8,128)(2,1)}, bf16[256,1280]{1,0:T(8,128)(2,1)}) custom-call(bf16[256,1280]{1,0:T(8,128)(2,1)} %get-tuple-element.6.a, bf16[256,1280]{1,0:T(8,128)(2,1)} %get-tuple-element.7.b, bf16[256,1280]{1,0:T(8,128)(2,1)} %get-tuple-element.8.c), custom_call_target="tpu_custom_call" | custom-call | tf_op jit(solution)/shard_map/pallas_call | solution.py:489

commit v6 on v5

--- a/solution.py
+++ b/solution.py
@@ -203,54 +203,41 @@
             device_id=before1, device_id_type=MESH,
         )
 
-    def group(f, d):
-        h = lax.rem(y + d + 4, 4)
+    def product(f, h):
         for xx in range(4):
             wait_w(slot(h, 1 - core, f, xx))
-        mine = h // 2 == pair
-        j = lax.rem(h, 2)
-
-        def product():
-            total = 0.0
-            for c in range(2):
-                rows = pl.ds(pl.multiple_of(slot(h, c, f, 0) * shard, 16), part)
-                total += dot(wbuf[rows, :], dl[c], NT)
-            return total
-
-        @pl.when(mine)
-        def _():
-            keep[j, f] = product()
-
-        @pl.when(jnp.logical_not(mine))
-        def _():
-            send1[j, f] = product().astype(jnp.bfloat16)
+        total = 0.0
+        for c in range(2):
+            rows = pl.ds(pl.multiple_of(slot(h, c, f, 0) * shard, 16), part)
+            total += dot(wbuf[rows, :], dl[c], NT)
+        return total
+
+    def send_groups(f):
+        for h in (3 - zlo, flip2):
+            j = lax.rem(h, 2)
+            send1[j, f] = product(f, h).astype(jnp.bfloat16)
             one_copy(j, f).start()
 
-    def combine(f, d):
-        h = lax.rem(y + d + 4, 4)
-        j = lax.rem(h, 2)
-
-        def total():
+    def keep_groups(f):
+        for h in (flip1, zlo):
+            keep[lax.rem(h, 2), f] = product(f, h)
+
+    def combine(f):
+        def total(j):
             one_copy(j, f).wait_recv()
             return (keep[j, f] + recv1[j, f].astype(jnp.float32)).astype(jnp.bfloat16)
 
-        @pl.when(h == zlo)
-        def _():
-            do_parts[half, f] = total()
-            do_copy(half, f).start()
-
-        @pl.when(h == flip1)
-        def _():
-            send2[f] = total()
-            two_copy(f).start()
-            side_copy(f).start()
+        send2[f] = total(1 - half)
+        two_copy(f).start()
+        side_copy(f).start()
+        do_parts[half, f] = total(half)
+        do_copy(half, f).start()
 
     def arrange(parts, whole):
         for m in range(16):
             xx, f, b = m // 4, m // 2 % 2, m % 2
             whole[m * shard:(m + 1) * shard, :] = parts[b, f, xx * shard:(xx + 1) * shard, :]
 
-    e = 2 * lax.rem(y, 2) - 1
     dl_copy = pltpu.make_async_remote_copy(
         dl_hbm, dl.at[half], dl_sem.at[0], dl_sem.at[1], device_id=side1, device_id_type=MESH
     )
@@ -278,43 +265,34 @@
     log_copy.start()
     second_near(zf, -1)
     second_near(zf, 2)
+    first_near(zg)
     second_far(zf, 0)
-    first_near(zg)
-    dl_arrival.wait_recv()
-    group(zf, 0)
     second_far(zf, 1)
     second_far(zf, -1)
-    group(zf, e)
-    group(zf, -e)
     first_far(zg)
     second_far(zf, 2)
-    group(zf, 2)
+    dl_arrival.wait_recv()
+    send_groups(zf)
+    second_near(zg, 0)
+    second_near(zg, 1)
+    keep_groups(zf)
+    second_near(zg, -1)
+    second_near(zg, 2)
+
     def turn(t, carry):
         c = pl.ds(pl.multiple_of(t * HD, HD), HD)
         ao_t[c, :] = ao[:, c].T
         return carry
 
     lax.fori_loop(0, width // HD, turn, 0)
-    second_near(zg, 0)
-    second_near(zg, 1)
-    combine(zf, 0)
-    combine(zf, e)
-    second_near(zg, -1)
     second_far(zg, 0)
-    group(zg, 0)
-    second_near(zg, 2)
-    combine(zf, -e)
-    combine(zf, 2)
     second_far(zg, 1)
     second_far(zg, -1)
-    group(zg, e)
-    group(zg, -e)
-    combine(zg, 0)
-    combine(zg, e)
     second_far(zg, 2)
-    group(zg, 2)
-    combine(zg, -e)
-    combine(zg, 2)
+    send_groups(zg)
+    combine(zf)
+    keep_groups(zg)
+    combine(zg)
     for f in range(2):
         two_arrival(f).wait_recv()
     arrange(do_parts, do)

time: 128 us -> 123 us (0.961); the launches traced: 126 us -> 123 us
  Pallas kernels: 125 us -> 122 us
    pallas_call x1, Pallas kernels: 122 us -> 119 us  [on_device(): pl.pallas_call(kernel, out_shape=(out, out, out), in_specs=[pl.BlockSpec(...]
where the time goes in v6:
time: 123 us
  Pallas kernels  122 us (99%)
    pallas_call x1, Pallas kernels, on_device(): pl.pallas_call(kernel, out_shape=(out, out, out), in_specs=[pl.BlockSpec(...  119 us

profile of v6, /device:TPU:32, one launch (start us, length us, event | category | flops | bytes accessed | tf_op | source)
XLA Modules:
  0.0 122.5 jit_solution(11445615574513227719)
XLA Ops:
  0.6 119.5 %shard_map.94 = (bf16[256,1280]{1,0:T(8,128)(2,1)}, bf16[256,1280]{1,0:T(8,128)(2,1)}, bf16[256,1280]{1,0:T(8,128)(2,1)}) custom-call(bf16[256,1280]{1,0:T(8,128)(2,1)} %q_hbm.1, bf16[256,1280]{1,0:T(8,128)(2,1)} %k_hbm.1, bf16[256,1280]{1,0:T(8,128)(2,1)} %v_hbm.1, bf16[256,1280]{1,0:T(8,128)(2,1)} %ao_hbm.1, f32[10,256]{1,0:T(8,128)} %log_hbm.1, ...), custom_call_target="tpu_custom_call" | custom-call | tf_op jit(solution)/shard_map/pallas_call | solution.py:457
  120.1 2.4 %shard_map.95 = (bf16[256,1280]{1,0:T(8,128)(2,1)}, bf16[256,1280]{1,0:T(8,128)(2,1)}, bf16[256,1280]{1,0:T(8,128)(2,1)}) custom-call(bf16[256,1280]{1,0:T(8,128)(2,1)} %get-tuple-element.6.a, bf16[256,1280]{1,0:T(8,128)(2,1)} %get-tuple-element.7.b, bf16[256,1280]{1,0:T(8,128)(2,1)} %get-tuple-element.8.c), custom_call_target="tpu_custom_call" | custom-call | tf_op jit(solution)/shard_map/pallas_call | solution.py:467

commit v7 on v6

--- a/solution.py
+++ b/solution.py
@@ -213,7 +213,7 @@
         return total
 
     def send_groups(f):
-        for h in (3 - zlo, flip2):
+        for h in (flip2, 3 - zlo):
             j = lax.rem(h, 2)
             send1[j, f] = product(f, h).astype(jnp.bfloat16)
             one_copy(j, f).start()
@@ -249,10 +249,6 @@
     begin(zf)
     first_near(zf)
     first_far(zf)
-    second_near(zf, 0)
-    second_near(zf, 1)
-    wait_w(at(zg, 0, 0))
-    begin(zg)
     for c in loads:
         c.wait()
     q_copy = pltpu.make_async_remote_copy(
@@ -263,6 +259,10 @@
     )
     q_copy.start()
     log_copy.start()
+    second_near(zf, 0)
+    second_near(zf, 1)
+    wait_w(at(zg, 0, 0))
+    begin(zg)
     second_near(zf, -1)
     second_near(zf, 2)
     first_near(zg)

time: 123 us -> 121 us (0.984)
  Pallas kernels: 122 us -> 120 us
    pallas_call x1, Pallas kernels: 119 us -> 118 us  [on_device(): pl.pallas_call(kernel, out_shape=(out, out, out), in_specs=[pl.BlockSpec(...]
where the time goes in v7:
time: 121 us
  Pallas kernels  120 us (99%)
    pallas_call x1, Pallas kernels, on_device(): pl.pallas_call(kernel, out_shape=(out, out, out), in_specs=[pl.BlockSpec(...  118 us

profile of v7, /device:TPU:32, one launch (start us, length us, event | category | flops | bytes accessed | tf_op | source)
XLA Modules:
  0.0 121.0 jit_solution(7092673525287432292)
XLA Ops:
  0.6 118.0 %shard_map.94 = (bf16[256,1280]{1,0:T(8,128)(2,1)}, bf16[256,1280]{1,0:T(8,128)(2,1)}, bf16[256,1280]{1,0:T(8,128)(2,1)}) custom-call(bf16[256,1280]{1,0:T(8,128)(2,1)} %q_hbm.1, bf16[256,1280]{1,0:T(8,128)(2,1)} %k_hbm.1, bf16[256,1280]{1,0:T(8,128)(2,1)} %v_hbm.1, bf16[256,1280]{1,0:T(8,128)(2,1)} %ao_hbm.1, f32[10,256]{1,0:T(8,128)} %log_hbm.1, ...), custom_call_target="tpu_custom_call" | custom-call | tf_op jit(solution)/shard_map/pallas_call | solution.py:457
  118.6 2.4 %shard_map.95 = (bf16[256,1280]{1,0:T(8,128)(2,1)}, bf16[256,1280]{1,0:T(8,128)(2,1)}, bf16[256,1280]{1,0:T(8,128)(2,1)}) custom-call(bf16[256,1280]{1,0:T(8,128)(2,1)} %get-tuple-element.6.a, bf16[256,1280]{1,0:T(8,128)(2,1)} %get-tuple-element.7.b, bf16[256,1280]{1,0:T(8,128)(2,1)} %get-tuple-element.8.c), custom_call_target="tpu_custom_call" | custom-call | tf_op jit(solution)/shard_map/pallas_call | solution.py:467
